TPU v7x, 512 devices: a whole 4x8x8 slice. The times are simulated.
512 devices in a mesh: section: 4 (over y_hi), chan: 16 (over z, core), dp: 8 (over y_lo, x).
Axes of the slice: x: 4, y: 8 (y_hi: 4, y_lo: 2; y = y_hi * 2 + y_lo), z: 8, core: 2. Of those that a mesh axis runs over, the one named last changes fastest.
Arguments:
- images: bfloat16 [2560, 2048], P(('section', 'dp')), may hold values from -6 to 6
- conv_one: bfloat16 [3, 3, 2560, 5120], P(None, None, ('section', 'dp'), 'chan'), may hold values from -0.0390625 to 0.0390625
- conv_two: bfloat16 [3, 3, 5120, 5120], P(None, None, ('section', 'dp'), 'chan'), may hold values from -0.02734375 to 0.02734375
- mix_weight: bfloat16 [5120, 5120], P(('section', 'dp'), 'chan'), may hold values from -0.078125 to 0.078125
Outputs:
- block_out: bfloat16 [8, 64, 5120], P('dp', 'section', 'chan')
All inputs are finite; a program needn't handle non-finite values.
Results may differ from a plain program's by a relative error of at most 0.02.
Values may be sent and summed in bfloat16 or wider, within the bound.
A program may use at most 64 MiB of HBM per device.

v0:
```python
import jax
import jax.numpy as jnp
from jax import lax
from jax.sharding import PartitionSpec as P

HW = 16


def to_blocks(values, n_data, n_section):
    count, places, width = values.shape
    shaped = values.reshape(n_data, count // n_data, n_section, places // n_section, width)
    return shaped.transpose(2, 0, 1, 3, 4).reshape(-1, width)


def from_blocks(values, n_data, n_section, count, half):
    width = values.shape[1]
    places = half * half
    shaped = values.reshape(n_section, n_data, count // n_data, places // n_section, width)
    return shaped.transpose(1, 2, 0, 3, 4).reshape(count, half, half, width)


def per_device(images, conv_one, conv_two, mix_weight):
    n_section = lax.axis_size("section")
    n_data = lax.axis_size("dp")
    side = HW
    count = images.shape[1] // (side * side)
    half = side // 2
    rows = count * half * half
    in_local = images.shape[0]
    maps = images.reshape(in_local, count, side, side)
    padded = jnp.pad(maps, ((0, 0), (0, 0), (1, 1), (1, 1)))
    total = jnp.zeros((rows, conv_one.shape[3]), jnp.float32)
    for tap_a in range(3):
        for tap_b in range(3):
            window = padded[:, :, tap_a : tap_a + side : 2, tap_b : tap_b + side : 2].reshape(
                in_local, rows
            )
            total = total + lax.dot_general(
                window,
                conv_one[tap_a, tap_b],
                (((0,), (0,)), ((), ())),
                preferred_element_type=jnp.float32,
            )
    section_terms = to_blocks(total.reshape(count, half * half, -1), n_data, n_section)
    share_rows = rows // (n_section * n_data)
    summed = lax.psum(section_terms.astype(jnp.bfloat16), ("section", "dp"))
    skip = lax.dynamic_slice_in_dim(
        summed, lax.axis_index(("section", "dp")) * share_rows, share_rows, 0
    )
    rect_blocks = jnp.maximum(summed, 0)
    rectified = from_blocks(rect_blocks, n_data, n_section, count, half)
    padded_two = jnp.pad(rectified, ((0, 0), (1, 1), (1, 1), (0, 0)))
    inner = jnp.zeros((rows, conv_two.shape[2]), jnp.float32)
    for tap_a in range(3):
        for tap_b in range(3):
            window = padded_two[:, tap_a : tap_a + half, tap_b : tap_b + half, :].reshape(rows, -1)
            inner = inner + lax.dot_general(
                window,
                conv_two[tap_a, tap_b],
                (((1,), (1,)), ((), ())),
                preferred_element_type=jnp.float32,
            )
    inner_blocks = to_blocks(inner.reshape(count, half * half, -1), n_data, n_section)
    inner_sum = lax.psum(inner_blocks.astype(jnp.bfloat16), "chan").astype(jnp.float32)
    gated = jnp.maximum(inner_sum, 0.0).astype(jnp.bfloat16)
    mixed = lax.psum_scatter(
        jnp.dot(gated, mix_weight, preferred_element_type=jnp.float32).astype(jnp.bfloat16),
        ("section", "dp"),
        scatter_dimension=0,
        tiled=True,
    ).astype(jnp.float32)
    result = (mixed + skip.astype(jnp.float32)).astype(jnp.bfloat16)
    per_data = count // n_data
    return result.reshape(per_data, share_rows // per_data, -1)


def solution(mesh):
    in_specs = (
        P(("section", "dp"), None),
        P(None, None, ("section", "dp"), "chan"),
        P(None, None, ("section", "dp"), "chan"),
        P(("section", "dp"), "chan"),
    )
    out_specs = P("dp", "section", "chan")
    return jax.shard_map(
        per_device, mesh=mesh, in_specs=in_specs, out_specs=out_specs, check_vma=False
    )
```

profile of v0, /device:TPU:1, one launch (start us, length us, event | category | flops | bytes accessed | tf_op | source)
XLA Modules:
  0.0 518.6 jit_solution(15222768242337160034)
XLA Ops:
  6.5 0.0 copy-start
  6.5 0.0 all-reduce.5.cloned.1.call-start
  6.5 1.3 copy.6
  7.8 0.2 pad.8
  8.1 1.5 slice.106
  9.5 0.0 copy-start.2
  9.6 1.5 slice.108
  11.0 1.6 slice.110
  12.6 1.5 slice.112
  14.1 1.5 slice.114
  15.6 1.6 slice.116
  17.2 1.5 slice.118
  18.6 1.5 slice.120
  20.1 1.6 slice.122
  21.7 0.0 copy-done.2
  21.7 0.3 fusion.30
  22.0 0.3 convolution_add_fusion.7
  22.3 0.3 convolution_add_fusion.6
  22.6 0.3 convolution_add_fusion.5
  22.9 0.3 convolution_add_fusion.4
  23.2 0.3 convolution_add_fusion.3
  23.5 0.3 convolution_add_fusion.2
  23.8 0.3 convolution_add_fusion.1
  24.1 0.3 fusion
  24.4 0.2 copy.7
  24.6 0.8 copy.8
  25.4 0.0 all-reduce.5.cloned.1.call-update
  25.5 0.0 all-reduce.7.cloned.1.call-start
  25.5 157.3 %all-reduce.5.cloned.1.call-done = bf16[512,320]{1,0:T(8,128)(2,1)} async-done(((bf16[512,320]{1,0:T(8,128)(2,1)}), bf16[512,320]{1,0:T(8,128)(2,1)}) %all-reduce.5.cloned.1.call-update) | async-done | bytes 327696 | tf_op jit(solution)/shard_map/psum | solution.py:46
  182.8 1.0 broadcast_maximum_fusion
  183.9 0.0 copy-start.1
  183.9 0.5 pad_slice_fusion
  184.5 0.7 copy-done.1
  185.2 0.3 fusion.11
  185.5 0.3 convolution_add_fusion.15
  185.8 0.3 convolution_add_fusion.14
  186.0 0.3 convolution_add_fusion.13
  186.3 0.3 convolution_add_fusion.12
  186.6 0.3 convolution_add_fusion.11
  186.9 0.3 convolution_add_fusion.10
  187.2 0.3 convolution_add_fusion.9
  187.5 0.3 fusion.1
  187.8 0.1 copy.10
  187.9 0.7 copy.11
  188.7 0.0 all-reduce.7.cloned.1.call-update
  188.7 0.0 reduce-scatter.2.cloned.1.call-start
  188.7 116.9 %all-reduce.7.cloned.1.call-done = bf16[512,160]{1,0:T(8,128)(2,1)} async-done(((bf16[512,160]{1,0:T(8,128)(2,1)}), bf16[512,160]{1,0:T(8,128)(2,1)}) %all-reduce.7.cloned.1.call-update) | async-done | bytes 163856 | tf_op jit(solution)/shard_map/psum | solution.py:64
  305.7 0.0 copy-done
  305.7 2.0 convolution_convert_fusion
  307.7 0.0 reduce-scatter.2.cloned.1.call-update
  307.7 203.0 %reduce-scatter.2.cloned.1.call-done = bf16[16,320]{1,0:T(8,128)(2,1)} async-done(((bf16[512,320]{1,0:T(8,128)(2,1)}), bf16[16,320]{1,0:T(8,128)(2,1)}) %reduce-scatter.2.cloned.1.call-update) | async-done | bytes 10256 | tf_op jit(solution)/shard_map/reduce_scatter | solution.py:66
  510.7 1.3 fusion.41
  (1 shorter events, 0.0 us)
Async XLA Ops:
  6.5 299.1 %copy-start = (bf16[160,320]{1,0:T(8,128)(2,1)S(1)}, bf16[160,320]{1,0:T(8,128)(2,1)}, u32[]{:S(2)}) copy-start(bf16[160,320]{1,0:T(8,128)(2,1)} %param.7) | copy-start | bytes 307204
  6.5 176.3 %all-reduce.5.cloned.1.call-start = ((), (), s32[]{:S(2)}) async-start(), calls=%async_computation.1 | async-start | bytes 786432 | tf_op jit(solution)/shard_map/psum | solution.py:46
  9.5 12.2 %copy-start.2 = (bf16[3,3,80,320]{3,2,1,0:T(8,128)(2,1)S(1)}, bf16[3,3,80,320]{3,2,1,0:T(8,128)(2,1)}, u32[]{:S(2)}) copy-start(bf16[3,3,80,320]{3,2,1,0:T(8,128)(2,1)} %param.5) | copy-start | bytes 1382404
  25.5 280.2 %all-reduce.7.cloned.1.call-start = ((), (), s32[]{:S(2)}) async-start(), calls=%async_computation.2 | async-start | bytes 524288 | tf_op jit(solution)/shard_map/psum | solution.py:64
  183.9 1.2 copy-start.1
  188.7 322.1 %reduce-scatter.2.cloned.1.call-start = ((), (), s32[]{:S(2)}) async-start(), calls=%async_computation.3 | async-start | bytes 405504 | tf_op jit(solution)/shard_map/reduce_scatter | solution.py:66
Sparse Core Ops, SparseCore 0:
  25.6 157.2 all-reduce.4
  188.8 116.8 all-reduce.6
  310.1 200.6 reduce-scatter.1
where the time goes:
time: 523 us; the launch traced here: 519 us
  waiting for transfers between devices  477 us (91%)
  local copies, waits for them, and re-layouts  18.3 us (3%)
  between operations  13.4 us (3%)
  matrix products  7.12 us (1%)
    reduce_scatter x1, waiting for transfers between devices, per_device(): lax.psum_scatter(jnp.dot(gated, mix_weight, preferred_element_type=jnp.fl...  203 us
    psum x1, waiting for transfers between devices, per_device(): summed = lax.psum(section_terms.astype(jnp.bfloat16), ('section', 'dp'))  157 us
    psum x1, waiting for transfers between devices, per_device(): lax.psum(inner_blocks.astype(jnp.bfloat16), 'chan').astype(jnp.float32)  117 us
    slice x9, local copies, waits for them, and re-layouts, per_device(): padded[:, :, tap_a:tap_a + side:2, tap_b:tap_b + side:2]  13.6 us
  transfers between devices with their start and end apart: 3, of which 3 were waited for; matrix products, arithmetic and copies ran while one was open for 0% of the time, Pallas kernels for 0%

commit v1 on v0

v1 whole, which is shorter than its diff:
```python
import functools

import jax
import jax.numpy as jnp
from jax import lax
from jax.experimental import pallas as pl
from jax.experimental.pallas import tpu as pltpu
from jax.sharding import PartitionSpec as P

MESH = pl.DeviceIdType.MESH
BF16 = jnp.bfloat16
F32 = jnp.float32
NX, NY, NC = 4, 8, 16
HALVES = (0, 1)
ORDER = (1, 0)
FAR_FIRST = (8, 7, 9, 6, 10, 5, 11, 4, 12, 3, 13, 2, 14, 1, 15)
FORWARD = (1, 7, 2, 6, 3, 5, 4)


def nt(a, b):
    return lax.dot_general(a, b, (((1,), (1,)), ((), ())), preferred_element_type=F32)


def selection():
    row = lax.broadcasted_iota(jnp.int32, (192, 768), 0)
    col = lax.broadcasted_iota(jnp.int32, (192, 768), 1)
    a, i, j = row >> 6, (row >> 3) & 7, row & 7
    b, place = col >> 8, col & 255
    wanted = (2 * i + a - 1) * 16 + 2 * j + b - 1
    inside = jnp.logical_or(j > 0, b > 0)
    hit = jnp.logical_and(wanted == place, inside)
    return jnp.where(hit, 1.0, 0.0).astype(BF16)


def kernel(
    images, conv_one, conv_two, mix_weight, out,
    maps, w1, w2, wm, sel, lhs, snd1, rcvx1, ybuf1, rcvy1, hid, zsnd, rcvz, gat,
    snd3, rcvx3, ybuf3, rcvy3, load_sem, send_sem, rx1, ry1, ay, ax, rz, az, rx3, ry3,
):
    s, c, d = lax.axis_index("section"), lax.axis_index("chan"), lax.axis_index("dp")
    x = d % NX
    y = s * 2 + d // NX
    par = y % 2
    quarter = y // 2

    def at_x(k):
        return (s, c, (d // NX) * NX + (x + k) % NX)

    def at_y(k):
        to = (y + k) % NY
        return (to // 2, c, (to % 2) * NX + x)

    def at_c(k):
        return (s, (c + k) % NC, d)

    loads = [
        pltpu.make_async_copy(images.at[:, pl.ds(pl.multiple_of(par * 1024, 1024), 1024)], maps.at[0], load_sem.at[0]),
        pltpu.make_async_copy(conv_one, w1, load_sem.at[2]),
        pltpu.make_async_copy(images.at[:, pl.ds(pl.multiple_of((1 - par) * 1024, 1024), 1024)], maps.at[1], load_sem.at[1]),
        pltpu.make_async_copy(conv_two, w2, load_sem.at[3]),
        pltpu.make_async_copy(mix_weight, wm, load_sem.at[4]),
    ]
    for copy in loads:
        copy.start()

    barrier = pltpu.get_barrier_semaphore()
    for k in (4, 3, 5, 2, 6, 1, 7):
        pl.semaphore_signal(barrier, 1, device_id=at_y(k), device_id_type=MESH)
    for k in FAR_FIRST:
        pl.semaphore_signal(barrier, 1, device_id=at_c(k), device_id_type=MESH)
    for k in range(1, NX):
        pl.semaphore_signal(barrier, 1, device_id=at_x(k), device_id_type=MESH)

    def send(src, dst, which, sem, to):
        pltpu.make_async_remote_copy(
            src_ref=src, dst_ref=dst, send_sem=send_sem.at[which], recv_sem=sem, device_id=to, device_id_type=MESH
        ).start()

    def wait(ref, sem):
        pltpu.make_async_copy(ref, ref, sem).wait()

    def distance(g, r):
        return (4 - g + 2 * r) % NY

    def send_x(g, snd, rcvx, rx, which):
        for r in range(4):
            q = ((y + distance(g, r)) % NY) // 2
            for k in (2, 1, 3):
                send(snd.at[g, (x + k) % NX, q], rcvx.at[g, r, k - 1], which, rx.at[g, r], at_x(k))

    def send_y(g, snd, rcvx, rx, ybuf, rcvy, ry, which):
        own = None
        for r in range(4):
            k = distance(g, r)
            q = ((y + k) % NY) // 2
            wait(rcvx.at[g, r], rx.at[g, r])
            total = snd[g, x, q].astype(F32)
            for other in range(NX - 1):
                total = total + rcvx[g, r, other].astype(F32)
            if k == 0:
                own = total
            else:
                ybuf[g, r] = total.astype(BF16)
                send(ybuf.at[g, r], rcvy.at[k - 1], which, ry, at_y(k))
        return own

    sel[...] = selection()
    zero = jnp.zeros((80, 256), BF16)
    for g in HALVES:
        loads[0 if g == 0 else 2].wait()
        for n in range(4):
            one = maps[g, :, n * 256 : (n + 1) * 256]
            spread = jnp.concatenate(
                [
                    jnp.concatenate([one, zero, zero], 1),
                    jnp.concatenate([zero, one, zero], 1),
                    jnp.concatenate([zero, zero, one], 1),
                ],
                0,
            )
            windows = nt(sel[...], spread).astype(BF16)
            for a in range(3):
                lhs[a, n * 64 : (n + 1) * 64] = windows[a * 64 : (a + 1) * 64]
        if g == 0:
            loads[1].wait()
        total = jnp.zeros((256, 320), F32)
        for a in range(3):
            total = total + jnp.dot(lhs[a], w1[a].reshape(240, 320), preferred_element_type=F32)
        snd1[g] = total.astype(BF16).reshape(4, 4, 16, 320)
        if g == 0:
            pl.semaphore_wait(barrier, (NX - 1) + (NY - 1) + (NC - 1))
        send_x(g, snd1, rcvx1, rx1, 0)

    own = None
    for g in HALVES:
        got = send_y(g, snd1, rcvx1, rx1, ybuf1, rcvy1, ry1, 1)
        own = got if own is None else own
    wait(rcvy1, ry1)
    for k in range(NY - 1):
        own = own + rcvy1[k].astype(F32)
    mine = own.astype(BF16)
    hid[0, x, quarter] = mine

    for k in (4, 3, 5, 2, 6, 1, 7):
        here = hid.at[0, x, quarter]
        send(here, hid.at[k % 2, x, quarter], 2, ay.at[k - 1], at_y(k))

    def forward(g, q):
        for k in (2, 1, 3):
            send(hid.at[g, x, q], hid.at[g, x, q], 3, ax.at[g], at_x(k))

    forward(0, quarter)
    for k in FORWARD:
        q = ((y - k + NY) % NY) // 2
        wait(hid.at[k % 2, x, q], ay.at[k - 1])
        forward(k % 2, q)

    loads[3].wait()
    for g in ORDER:
        wait(hid.at[g, 0:3], ax.at[g])
        rect = jnp.maximum(hid[g].reshape(256, 320).astype(F32), 0.0).reshape(32, 8, 320)
        place = lax.broadcasted_iota(jnp.int32, (32, 8, 320), 1)
        left = jnp.where(place == 0, 0.0, pltpu.roll(rect, 1, 1))
        right = jnp.where(place == 7, 0.0, pltpu.roll(rect, 7, 1))
        shifted = [v.reshape(256, 320).astype(BF16) for v in (left, rect, right)]
        parts = []
        for a in range(3):
            acc = jnp.zeros((256, 160), F32)
            for b in range(3):
                acc = acc + nt(shifted[b], w2[a, b])
            parts.append(acc.reshape(4, 64, 160))
        gap = jnp.zeros((4, 8, 160), F32)
        inner = (
            parts[1]
            + jnp.concatenate([gap, parts[0][:, :56]], 1)
            + jnp.concatenate([parts[2][:, 8:], gap], 1)
        )
        zsnd[g] = inner.astype(BF16).reshape(16, 16, 160)
        for k in FAR_FIRST:
            send(zsnd.at[g, (c + k) % NC], rcvz.at[g, k - 1], 4, rz.at[g], at_c(k))

    for g in ORDER:
        wait(rcvz.at[g], rz.at[g])
        total = zsnd[g, c].astype(F32)
        for k in range(NC - 1):
            total = total + rcvz[g, k].astype(F32)
        gat[g, c] = jnp.maximum(total, 0.0).astype(BF16)
        for k in FAR_FIRST:
            send(gat.at[g, c], gat.at[g, c], 4, az.at[g], at_c(k))

    loads[4].wait()
    for g in ORDER:
        wait(gat.at[g, 0 : NC - 1], az.at[g])
        mixed = jnp.dot(gat[g].reshape(256, 160), wm[...], preferred_element_type=F32)
        snd3[g] = mixed.astype(BF16).reshape(4, 4, 16, 320)
        send_x(g, snd3, rcvx3, rx3, 0)
    own = None
    for g in ORDER:
        got = send_y(g, snd3, rcvx3, rx3, ybuf3, rcvy3, ry3, 1)
        own = got if own is None else own
    wait(rcvy3, ry3)
    for k in range(NY - 1):
        own = own + rcvy3[k].astype(F32)
    out[0] = (own + mine.astype(F32)).astype(BF16)

    for _ in range(2):
        wait(snd1.at[:, 0:3], send_sem.at[0])
        wait(rcvy1, send_sem.at[1])
        wait(rcvz, send_sem.at[4])
    wait(rcvy1, send_sem.at[2])
    wait(snd1.at[:, 0:3], send_sem.at[3])


def solution(mesh):
    def step(images, conv_one, conv_two, mix_weight):
        chunk = (16, 320)
        vmem = functools.partial(pltpu.VMEM, dtype=BF16)
        dma = pltpu.SemaphoreType.DMA
        return pl.pallas_call(
            kernel,
            out_shape=jax.ShapeDtypeStruct((1, *chunk), BF16),
            in_specs=[pl.BlockSpec(memory_space=pl.ANY)] * 4,
            out_specs=pl.BlockSpec(memory_space=pltpu.VMEM),
            scratch_shapes=[
                vmem((2, 80, 1024)),
                vmem((3, 3, 80, 320)),
                vmem((3, 3, 160, 320)),
                vmem((160, 320)),
                vmem((192, 768)),
                vmem((3, 256, 240)),
                vmem((2, NX, 4, *chunk)),
                vmem((2, 4, NX - 1, *chunk)),
                vmem((2, 4, *chunk)),
                vmem((NY - 1, *chunk)),
                vmem((2, NX, 4, *chunk)),
                vmem((2, NC, 16, 160)),
                vmem((2, NC - 1, 16, 160)),
                vmem((2, NC, 16, 160)),
                vmem((2, NX, 4, *chunk)),
                vmem((2, 4, NX - 1, *chunk)),
                vmem((2, 4, *chunk)),
                vmem((NY - 1, *chunk)),
                dma((5,)),
                dma((5,)),
                dma((2, 4)),
                dma,
                dma((NY - 1,)),
                dma((2,)),
                dma((2,)),
                dma((2,)),
                dma((2, 4)),
                dma,
            ],
            compiler_params=pltpu.CompilerParams(
                collective_id=0, has_side_effects=True, vmem_limit_bytes=48 * 2**20
            ),
            name="block",
        )(images, conv_one, conv_two, mix_weight)

    in_specs = (
        P(("section", "dp"), None),
        P(None, None, ("section", "dp"), "chan"),
        P(None, None, ("section", "dp"), "chan"),
        P(("section", "dp"), "chan"),
    )
    out_specs = P("dp", "section", "chan")
    return jax.shard_map(step, mesh=mesh, in_specs=in_specs, out_specs=out_specs, check_vma=False)
```

time: 523 us -> 62.3 us (0.12)
  waiting for transfers between devices: 477 us -> 0 us
  Pallas kernels: 0 us -> 56.7 us
  local copies, waits for them, and re-layouts: 18.3 us -> 4.77 us
  between operations: 13.4 us -> 0.01 us
  matrix products: 7.12 us -> 0 us
    psum x2 -> x0, waiting for transfers between devices: 274 us -> none  [the longest x1 157 us: per_device(): summed = lax.psum(section_terms.astype(jnp.bfloat16), ('section', 'dp'))]
    reduce_scatter x1 -> x0, waiting for transfers between devices: 203 us -> none  [per_device(): lax.psum_scatter(jnp.dot(gated, mix_weight, preferred_element_type=jnp.fl...]
    pallas_call x0 -> x1, Pallas kernels: none -> 56.7 us  [step(): pl.pallas_call(kernel, out_shape=jax.ShapeDtypeStruct((1, *chunk), BF16),...]
    slice x10 -> x0, local copies, waits for them, and re-layouts: 14.1 us -> none  [the longest x9 13.6 us: per_device(): padded[:, :, tap_a:tap_a + side:2, tap_b:tap_b + side:2]]
    dot_general x19 -> x0, matrix products: 7.12 us -> none  [the longest x9 2.6 us: per_device(): lax.dot_general(window, conv_one[tap_a, tap_b], (((0,), (0,)), ((), ())),...]
  transfers between devices with their start and end apart: 3 -> 0, of which waited for: 3 -> 0; matrix products, arithmetic and copies ran while one was open for 0% -> 0% of each run, Pallas kernels for 0% -> 0%
where the time goes in v1:
time: 62.3 us; the launch traced here: 61.5 us
  Pallas kernels  56.7 us (91%)
  local copies, waits for them, and re-layouts  4.77 us (8%)
    pallas_call x1, Pallas kernels, step(): pl.pallas_call(kernel, out_shape=jax.ShapeDtypeStruct((1, *chunk), BF16),...  56.7 us
    unnamed x9, local copies, waits for them, and re-layouts  4.77 us

profile of v1, /device:TPU:1, one launch (start us, length us, event | category | flops | bytes accessed | tf_op | source)
XLA Modules:
  0.0 61.5 jit_solution(15435643456833771512)
XLA Ops:
  0.0 0.0 copy-start
  0.0 1.2 %copy-done = bf16[3,3,160,320]{3,2,1,0:T(8,128)(2,1)S(1)} copy-done((bf16[3,3,160,320]{3,2,1,0:T(8,128)(2,1)S(1)}, bf16[3,3,160,320]{3,2,1,0:T(8,128)(2,1)}, u32[]{:S(2)}) %copy-start) | copy-done | bytes 921624
  1.2 0.0 copy-start.1
  1.2 1.0 %copy-done.1 = bf16[3,3,80,320]{3,2,1,0:T(8,128)(2,1)S(1)} copy-done((bf16[3,3,80,320]{3,2,1,0:T(8,128)(2,1)S(1)}, bf16[3,3,80,320]{3,2,1,0:T(8,128)(2,1)}, u32[]{:S(2)}) %copy-start.1) | copy-done | bytes 460824
  2.3 0.0 copy-start.2
  2.3 1.0 %copy-done.2 = bf16[80,2048]{1,0:T(8,128)(2,1)S(1)} copy-done((bf16[80,2048]{1,0:T(8,128)(2,1)S(1)}, bf16[80,2048]{1,0:T(8,128)(2,1)}, u32[]{:S(2)}) %copy-start.2) | copy-done | bytes 327704
  3.3 0.0 copy-start.3
  3.3 0.9 %copy-done.3 = bf16[160,320]{1,0:T(8,128)(2,1)S(1)} copy-done((bf16[160,320]{1,0:T(8,128)(2,1)S(1)}, bf16[160,320]{1,0:T(8,128)(2,1)}, u32[]{:S(2)}) %copy-start.3) | copy-done | bytes 102424
  4.2 56.7 %block.1 = bf16[1,16,320]{2,1,0:T(8,128)(2,1)S(1)} custom-call(bf16[80,2048]{1,0:T(8,128)(2,1)S(1)} %copy-done.2, bf16[3,3,80,320]{3,2,1,0:T(8,128)(2,1)S(1)} %copy-done.1, bf16[3,3,160,320]{3,2,1,0:T(8,128)(2,1)S(1)} %copy-done, bf16[160,320]{1,0:T(8,128)(2,1)S(1)} %copy-done.3), custom_call_target="tpu_custom_call" | custom-call | tf_op jit(solution)/shard_map/block/pallas_call | solution.py:219
  60.9 0.6 copy.6
Async XLA Ops:
  0.0 1.2 %copy-start = (bf16[3,3,160,320]{3,2,1,0:T(8,128)(2,1)S(1)}, bf16[3,3,160,320]{3,2,1,0:T(8,128)(2,1)}, u32[]{:S(2)}) copy-start(bf16[3,3,160,320]{3,2,1,0:T(8,128)(2,1)} %conv_two.1) | copy-start | bytes 2764804
  1.2 1.1 %copy-start.1 = (bf16[3,3,80,320]{3,2,1,0:T(8,128)(2,1)S(1)}, bf16[3,3,80,320]{3,2,1,0:T(8,128)(2,1)}, u32[]{:S(2)}) copy-start(bf16[3,3,80,320]{3,2,1,0:T(8,128)(2,1)} %conv_one.1) | copy-start | bytes 1382404
  2.3 1.0 %copy-start.2 = (bf16[80,2048]{1,0:T(8,128)(2,1)S(1)}, bf16[80,2048]{1,0:T(8,128)(2,1)}, u32[]{:S(2)}) copy-start(bf16[80,2048]{1,0:T(8,128)(2,1)} %images.1) | copy-start | bytes 983044
  3.3 0.9 %copy-start.3 = (bf16[160,320]{1,0:T(8,128)(2,1)S(1)}, bf16[160,320]{1,0:T(8,128)(2,1)}, u32[]{:S(2)}) copy-start(bf16[160,320]{1,0:T(8,128)(2,1)} %mix_weight.1) | copy-start | bytes 307204

commit v2 on v1

v2 whole, which is shorter than its diff:
```python
import functools

import jax
import jax.numpy as jnp
from jax import lax
from jax.experimental import pallas as pl
from jax.experimental.pallas import tpu as pltpu
from jax.sharding import PartitionSpec as P

MESH = pl.DeviceIdType.MESH
BF16 = jnp.bfloat16
F32 = jnp.float32
NX, NY, NZ = 4, 8, 8
CHUNK = (16, 320)
SUBS = 2
IMGS = 4 // SUBS
ZROWS = 32 // SUBS
FAR = (4, 3, 5, 2, 6, 1, 7)


def nt(a, b):
    return lax.dot_general(a, b, (((1,), (1,)), ((), ())), preferred_element_type=F32)


def selection():
    row = lax.broadcasted_iota(jnp.int32, (192, 768), 0)
    col = lax.broadcasted_iota(jnp.int32, (192, 768), 1)
    a, i, j = row >> 6, (row >> 3) & 7, row & 7
    b, place = col >> 8, col & 255
    wanted = (2 * i + a - 1) * 16 + 2 * j + b - 1
    inside = jnp.logical_or(j > 0, b > 0)
    hit = jnp.logical_and(wanted == place, inside)
    return jnp.where(hit, 1.0, 0.0).astype(BF16)


def kernel(
    images, conv_one, conv_two, mix_weight, out,
    maps, w1, w2, wm, sel, lhs, snd1, rcvx1, ybuf1, rcvy1, mine, agbuf, hid, zsnd, rcvz, gat,
    snd3, rcvx3, ybuf3, rcvy3, load_sem, send_sem, swap_sem, rx1, ry1, ay, ax, rz, az, rx3, ry3,
):
    s, c, d = lax.axis_index("section"), lax.axis_index("chan"), lax.axis_index("dp")
    x = d % NX
    y = s * 2 + d // NX
    z = c // 2
    core = c % 2
    par = y % 2
    quarter = y // 2

    def at_x(k, to_core):
        return (s, z * 2 + to_core, (d // NX) * NX + (x + k) % NX)

    def at_y(k):
        to = (y + k) % NY
        return (to // 2, c, (to % 2) * NX + x)

    def at_z(k):
        return (s, ((z + k) % NZ) * 2 + core, d)

    partner = (s, z * 2 + 1 - core, d)

    barrier = pltpu.get_barrier_semaphore()

    def greet(to):
        pl.semaphore_signal(barrier, 1, device_id=to, device_id_type=MESH)

    for k in FAR:
        greet(at_y(k))
        greet(at_z(k))
    for k in (2, 1, 3):
        greet(at_x(k, core))
        greet(at_x(k, 1 - core))
    greet(partner)

    loads = [
        pltpu.make_async_copy(images.at[:, pl.ds(pl.multiple_of((1 - par) * 1024, 1024), 1024)], maps.at[0], load_sem.at[0]),
        pltpu.make_async_copy(conv_one, w1, load_sem.at[2]),
        pltpu.make_async_copy(images.at[:, pl.ds(pl.multiple_of(par * 1024, 1024), 1024)], maps.at[1], load_sem.at[1]),
        pltpu.make_async_copy(conv_two, w2.at[core], load_sem.at[3]),
        pltpu.make_async_copy(mix_weight, wm.at[core], load_sem.at[4]),
    ]
    for copy in loads:
        copy.start()

    def send(src, dst, which, sem, to):
        pltpu.make_async_remote_copy(
            src_ref=src, dst_ref=dst, send_sem=send_sem.at[which], recv_sem=sem, device_id=to, device_id_type=MESH
        ).start()

    def wait(ref, sem):
        pltpu.make_async_copy(ref, ref, sem).wait()

    sel[...] = selection()
    zero = jnp.zeros((80, 256), BF16)
    for g in range(2):
        loads[0 if g == 0 else 2].wait()
        for n in range(4):
            one = maps[g, :, n * 256 : (n + 1) * 256]
            spread = jnp.concatenate(
                [
                    jnp.concatenate([one, zero, zero], 1),
                    jnp.concatenate([zero, one, zero], 1),
                    jnp.concatenate([zero, zero, one], 1),
                ],
                0,
            )
            windows = nt(sel[...], spread).astype(BF16)
            for a in range(3):
                lhs[a, n * 64 : (n + 1) * 64] = windows[a * 64 : (a + 1) * 64]
        if g == 0:
            loads[1].wait()
        total = jnp.zeros((256, 320), F32)
        for a in range(3):
            total = total + jnp.dot(lhs[a], w1[a].reshape(240, 320), preferred_element_type=F32)
        snd1[g] = total.astype(BF16).reshape(4, 4, *CHUNK)
        if g == 0:
            pl.semaphore_wait(barrier, 2 * (NX - 1) + 1 + (NY - 1) + (NZ - 1))
        for r in range(4):
            q = ((y + (4 - g + 2 * r) % NY) % NY) // 2
            for k in (2, 1, 3):
                send(snd1.at[g, (x + k) % NX, q], rcvx1.at[g, r, k - 1], 0, rx1.at[g, r], at_x(k, core))

    loads[3].wait()
    send(w2.at[core], w2.at[core], 5, swap_sem.at[0], partner)
    loads[4].wait()
    send(wm.at[core], wm.at[core], 6, swap_sem.at[1], partner)

    own = None
    for g in range(2):
        for r in range(4):
            k = (4 - g + 2 * r) % NY
            q = ((y + k) % NY) // 2
            wait(rcvx1.at[g, r], rx1.at[g, r])
            total = snd1[g, x, q].astype(F32)
            for other in range(NX - 1):
                total = total + rcvx1[g, r, other].astype(F32)
            if k == 0:
                own = total
            else:
                ybuf1[k - 1] = total.astype(BF16)
                send(ybuf1.at[k - 1], rcvy1.at[k - 1], 1, ry1, at_y(k))
    wait(rcvy1, ry1)
    for k in range(NY - 1):
        own = own + rcvy1[k].astype(F32)
    mine[...] = own.astype(BF16)

    for k in FAR:
        send(mine, agbuf.at[k - 1], 2, ay.at[k - 1], at_y(k))
    sub = x // IMGS
    for k in (0, 1, 7, 2, 6, 3, 5, 4):
        origin = (y - k + NY) % NY
        q = origin // 2
        to_core = 1 - origin % 2
        here = hid.at[core, x, q]
        if k == 0:
            src = mine
        else:
            src = agbuf.at[k - 1]
            wait(src, ay.at[k - 1])
        for kx in (2, 1, 3):
            send(src, here, 3, ax.at[sub], at_x(kx, to_core))

        @pl.when(to_core == core)
        def _():
            pltpu.make_async_copy(src, here, ax.at[sub]).start()

        @pl.when(to_core != core)
        def _():
            send(src, here, 3, ax.at[sub], partner)

    wait(w2.at[0], swap_sem.at[0])
    for t in range(SUBS):
        wait(hid.at[:, t * IMGS : (t + 1) * IMGS], ax.at[t])
        rows = IMGS * 64
        parts = [jnp.zeros((rows, 160), F32) for _ in range(3)]
        place = lax.broadcasted_iota(jnp.int32, (rows // 8, 8, 320), 1)
        for j in range(2):
            block = hid[j, t * IMGS : (t + 1) * IMGS].reshape(rows, 320)
            rect = jnp.maximum(block.astype(F32), 0.0).reshape(rows // 8, 8, 320)
            left = jnp.where(place == 0, 0.0, pltpu.roll(rect, 1, 1))
            right = jnp.where(place == 7, 0.0, pltpu.roll(rect, 7, 1))
            shifted = [v.reshape(rows, 320).astype(BF16) for v in (left, rect, right)]
            for a in range(3):
                for b in range(3):
                    parts[a] = parts[a] + nt(shifted[b], w2[j, a, b])
        parts = [v.reshape(IMGS, 64, 160) for v in parts]
        gap = jnp.zeros((IMGS, 8, 160), F32)
        inner = (
            parts[1]
            + jnp.concatenate([gap, parts[0][:, :56]], 1)
            + jnp.concatenate([parts[2][:, 8:], gap], 1)
        )
        zsnd[t] = inner.astype(BF16).reshape(NZ, ZROWS, 160)
        for k in FAR:
            send(zsnd.at[t, (z + k) % NZ], rcvz.at[t, k - 1], 4, rz.at[t], at_z(k))

    for t in range(SUBS):
        wait(rcvz.at[t], rz.at[t])
        total = zsnd[t, z].astype(F32)
        for k in range(NZ - 1):
            total = total + rcvz[t, k].astype(F32)
        gat[t, z] = jnp.maximum(total, 0.0).astype(BF16)
        for k in FAR:
            send(gat.at[t, z], gat.at[t, z], 4, az.at[t], at_z(k))

    wait(wm.at[0], swap_sem.at[1])
    for t in range(SUBS):
        wait(gat.at[t, 0 : NZ - 1], az.at[t])
        gated = gat[t].reshape(IMGS * 64, 160)
        for j in range(2):
            mixed = jnp.dot(gated, wm[j], preferred_element_type=F32).astype(BF16)
            snd3[j, t * IMGS : (t + 1) * IMGS] = mixed.reshape(IMGS, 4, *CHUNK)
    apart = (core + y) % 2
    for r in range(4):
        k = (4 - apart + 2 * r) % NY
        q = ((y + k) % NY) // 2
        for kx in (2, 1, 3):
            for j in range(2):
                send(snd3.at[j, (x + kx) % NX, q], rcvx3.at[k, kx], 0, rx3.at[k], at_x(kx, j))
        send(snd3.at[1 - core, x, q], rcvx3.at[k, 0], 0, rx3.at[k], partner)
        pltpu.make_async_copy(snd3.at[core, x, q], rcvx3.at[k, 0], rx3.at[k]).start()
    own = None
    for k in (*FAR, 0):
        wait(rcvx3.at[k], rx3.at[k])
        total = rcvx3[k, 0].astype(F32)
        for other in range(1, NX):
            total = total + rcvx3[k, other].astype(F32)
        if k == 0:
            own = total
        else:
            ybuf3[k - 1] = total.astype(BF16)
            send(ybuf3.at[k - 1], rcvy3.at[k - 1], 1, ry3, at_y(k))
    skip = agbuf[6 * (1 - par)]
    own = own + skip.astype(F32)
    wait(rcvy3, ry3)
    for k in range(NY - 1):
        own = own + rcvy3[k].astype(F32)
    out[0] = own.astype(BF16)

    for _ in range(4):
        wait(agbuf, send_sem.at[3])
    for _ in range(2):
        wait(snd1.at[:, 0:3], send_sem.at[0])
        wait(rcvy1, send_sem.at[1])
        wait(rcvz, send_sem.at[4])
    wait(hid.at[0, 0], send_sem.at[0])
    wait(agbuf, send_sem.at[2])
    wait(w2.at[0], send_sem.at[5])
    wait(wm.at[0], send_sem.at[6])


def solution(mesh):
    def step(images, conv_one, conv_two, mix_weight):
        vmem = functools.partial(pltpu.VMEM, dtype=BF16)
        dma = pltpu.SemaphoreType.DMA
        return pl.pallas_call(
            kernel,
            out_shape=jax.ShapeDtypeStruct((1, *CHUNK), BF16),
            in_specs=[pl.BlockSpec(memory_space=pl.ANY)] * 4,
            out_specs=pl.BlockSpec(memory_space=pltpu.VMEM),
            scratch_shapes=[
                vmem((2, 80, 1024)),
                vmem((3, 3, 80, 320)),
                vmem((2, 3, 3, 160, 320)),
                vmem((2, 160, 320)),
                vmem((192, 768)),
                vmem((3, 256, 240)),
                vmem((2, NX, 4, *CHUNK)),
                vmem((2, 4, NX - 1, *CHUNK)),
                vmem((NY - 1, *CHUNK)),
                vmem((NY - 1, *CHUNK)),
                vmem(CHUNK),
                vmem((NY - 1, *CHUNK)),
                vmem((2, NX, 4, *CHUNK)),
                vmem((SUBS, NZ, ZROWS, 160)),
                vmem((SUBS, NZ - 1, ZROWS, 160)),
                vmem((SUBS, NZ, ZROWS, 160)),
                vmem((2, NX, 4, *CHUNK)),
                vmem((NY, NX, *CHUNK)),
                vmem((NY - 1, *CHUNK)),
                vmem((NY - 1, *CHUNK)),
                dma((5,)),
                dma((7,)),
                dma((2,)),
                dma((2, 4)),
                dma,
                dma((NY - 1,)),
                dma((SUBS,)),
                dma((SUBS,)),
                dma((SUBS,)),
                dma((NY,)),
                dma,
            ],
            compiler_params=pltpu.CompilerParams(
                collective_id=0, has_side_effects=True, vmem_limit_bytes=60 * 2**20
            ),
            name="block",
        )(images, conv_one, conv_two, mix_weight)

    in_specs = (
        P(("section", "dp"), None),
        P(None, None, ("section", "dp"), "chan"),
        P(None, None, ("section", "dp"), "chan"),
        P(("section", "dp"), "chan"),
    )
    out_specs = P("dp", "section", "chan")
    return jax.shard_map(step, mesh=mesh, in_specs=in_specs, out_specs=out_specs, check_vma=False)
```

time: 62.3 us -> 57.3 us (0.920)
  local copies, waits for them, and re-layouts: 4.77 us -> 1.31 us
  Pallas kernels: 56.7 us -> 55.8 us
    unnamed x9 -> x1, local copies, waits for them, and re-layouts: 4.77 us -> 1.31 us
    pallas_call x1, Pallas kernels: 56.7 us -> 55.8 us  [step(): pl.pallas_call(kernel, out_shape=jax.ShapeDtypeStruct((1, *CHUNK), BF16),...]
where the time goes in v2:
time: 57.3 us; the launch traced here: 57.1 us
  Pallas kernels  55.8 us (97%)
  local copies, waits for them, and re-layouts  1.31 us (2%)
    pallas_call x1, Pallas kernels, step(): pl.pallas_call(kernel, out_shape=jax.ShapeDtypeStruct((1, *CHUNK), BF16),...  55.8 us
    unnamed x1, local copies, waits for them, and re-layouts  1.31 us

profile of v2, /device:TPU:1, one launch (start us, length us, event | category | flops | bytes accessed | tf_op | source)
XLA Modules:
  0.0 57.1 jit_solution(7750155041545465837)
XLA Ops:
  0.0 55.8 %block.1 = bf16[1,16,320]{2,1,0:T(8,128)(2,1)} custom-call(bf16[80,2048]{1,0:T(8,128)(2,1)} %images.1, bf16[3,3,80,320]{3,2,1,0:T(8,128)(2,1)} %conv_one.1, bf16[3,3,160,320]{3,2,1,0:T(8,128)(2,1)} %conv_two.1, bf16[160,320]{1,0:T(8,128)(2,1)} %mix_weight.1), custom_call_target="tpu_custom_call" | custom-call | tf_op jit(solution)/shard_map/block/pallas_call | solution.py:255
  55.8 1.3 %copy.6 = bf16[1,16,320]{2,1,0:T(8,128)(2,1)} copy(bf16[1,16,320]{2,1,0:T(8,128)(2,1)} %block.1) | data formatting | bytes 20480

commit v3 on v2

--- a/solution.py
+++ b/solution.py
@@ -114,7 +114,7 @@
         snd1[g] = total.astype(BF16).reshape(4, 4, *CHUNK)
         if g == 0:
             pl.semaphore_wait(barrier, 2 * (NX - 1) + 1 + (NY - 1) + (NZ - 1))
-        for r in range(4):
+        for r in (0, 1, 3, 2):
             q = ((y + (4 - g + 2 * r) % NY) % NY) // 2
             for k in (2, 1, 3):
                 send(snd1.at[g, (x + k) % NX, q], rcvx1.at[g, r, k - 1], 0, rx1.at[g, r], at_x(k, core))
@@ -126,7 +126,7 @@
 
     own = None
     for g in range(2):
-        for r in range(4):
+        for r in (0, 1, 3, 2):
             k = (4 - g + 2 * r) % NY
             q = ((y + k) % NY) // 2
             wait(rcvx1.at[g, r], rx1.at[g, r])
@@ -202,6 +202,7 @@
         for k in FAR:
             send(gat.at[t, z], gat.at[t, z], 4, az.at[t], at_z(k))
 
+    apart = (core + y) % 2
     wait(wm.at[0], swap_sem.at[1])
     for t in range(SUBS):
         wait(gat.at[t, 0 : NZ - 1], az.at[t])
@@ -209,17 +210,24 @@
         for j in range(2):
             mixed = jnp.dot(gated, wm[j], preferred_element_type=F32).astype(BF16)
             snd3[j, t * IMGS : (t + 1) * IMGS] = mixed.reshape(IMGS, 4, *CHUNK)
-    apart = (core + y) % 2
-    for r in range(4):
-        k = (4 - apart + 2 * r) % NY
-        q = ((y + k) % NY) // 2
-        for kx in (2, 1, 3):
-            for j in range(2):
-                send(snd3.at[j, (x + kx) % NX, q], rcvx3.at[k, kx], 0, rx3.at[k], at_x(kx, j))
-        send(snd3.at[1 - core, x, q], rcvx3.at[k, 0], 0, rx3.at[k], partner)
-        pltpu.make_async_copy(snd3.at[core, x, q], rcvx3.at[k, 0], rx3.at[k]).start()
+        for r in (0, 1, 3, 2):
+            k = (4 - apart + 2 * r) % NY
+            q = ((y + k) % NY) // 2
+            for to_x in range(t * IMGS, (t + 1) * IMGS):
+
+                @pl.when(x != to_x)
+                def _():
+                    kx = (to_x - x + NX) % NX
+                    for j in range(2):
+                        send(snd3.at[j, to_x, q], rcvx3.at[k, kx], 0, rx3.at[k], at_x(kx, j))
+
+                @pl.when(x == to_x)
+                def _():
+                    send(snd3.at[1 - core, to_x, q], rcvx3.at[k, 0], 0, rx3.at[k], partner)
+                    pltpu.make_async_copy(snd3.at[core, to_x, q], rcvx3.at[k, 0], rx3.at[k]).start()
+
     own = None
-    for k in (*FAR, 0):
+    for k in (4, 3, 6, 5, 2, 1, 7, 0):
         wait(rcvx3.at[k], rx3.at[k])
         total = rcvx3[k, 0].astype(F32)
         for other in range(1, NX):

time: 57.3 us -> 56.1 us (0.979)
  Pallas kernels: 55.8 us -> 54.6 us
    pallas_call x1, Pallas kernels: 55.8 us -> 54.6 us  [step(): pl.pallas_call(kernel, out_shape=jax.ShapeDtypeStruct((1, *CHUNK), BF16),...]
where the time goes in v3:
time: 56.1 us; the launch traced here: 56 us
  Pallas kernels  54.6 us (97%)
  local copies, waits for them, and re-layouts  1.31 us (2%)
    pallas_call x1, Pallas kernels, step(): pl.pallas_call(kernel, out_shape=jax.ShapeDtypeStruct((1, *CHUNK), BF16),...  54.6 us
    unnamed x1, local copies, waits for them, and re-layouts  1.31 us

profile of v3, /device:TPU:1, one launch (start us, length us, event | category | flops | bytes accessed | tf_op | source)
XLA Modules:
  0.0 56.0 jit_solution(16593711124801025013)
XLA Ops:
  0.0 54.6 %block.1 = bf16[1,16,320]{2,1,0:T(8,128)(2,1)} custom-call(bf16[80,2048]{1,0:T(8,128)(2,1)} %images.1, bf16[3,3,80,320]{3,2,1,0:T(8,128)(2,1)} %conv_one.1, bf16[3,3,160,320]{3,2,1,0:T(8,128)(2,1)} %conv_two.1, bf16[160,320]{1,0:T(8,128)(2,1)} %mix_weight.1), custom_call_target="tpu_custom_call" | custom-call | tf_op jit(solution)/shard_map/block/pallas_call | solution.py:263
  54.6 1.3 %copy.6 = bf16[1,16,320]{2,1,0:T(8,128)(2,1)} copy(bf16[1,16,320]{2,1,0:T(8,128)(2,1)} %block.1) | data formatting | bytes 20480

commit v4 on v3

--- a/solution.py
+++ b/solution.py
@@ -199,8 +199,11 @@
         for k in range(NZ - 1):
             total = total + rcvz[t, k].astype(F32)
         gat[t, z] = jnp.maximum(total, 0.0).astype(BF16)
-        for k in FAR:
-            send(gat.at[t, z], gat.at[t, z], 4, az.at[t], at_z(k))
+        for to_z in (0, 1, 2, 3, 7, 6, 5, 4):
+
+            @pl.when(to_z != z)
+            def _():
+                send(gat.at[t, z], gat.at[t, z], 4, az.at[t], at_z(to_z - z + NZ))
 
     apart = (core + y) % 2
     wait(wm.at[0], swap_sem.at[1])

time: 56.1 us -> 55.8 us (level)
  no operation moved by 1% of the time
where the time goes in v4:
time: 55.8 us; the launch traced here: 55.6 us
  Pallas kernels  54.3 us (97%)
  local copies, waits for them, and re-layouts  1.31 us (2%)
    pallas_call x1, Pallas kernels, step(): pl.pallas_call(kernel, out_shape=jax.ShapeDtypeStruct((1, *CHUNK), BF16),...  54.3 us
    unnamed x1, local copies, waits for them, and re-layouts  1.31 us

profile of v4, /device:TPU:1, one launch (start us, length us, event | category | flops | bytes accessed | tf_op | source)
XLA Modules:
  0.0 55.6 jit_solution(14931322094528193865)
XLA Ops:
  0.0 54.3 %block.1 = bf16[1,16,320]{2,1,0:T(8,128)(2,1)} custom-call(bf16[80,2048]{1,0:T(8,128)(2,1)} %images.1, bf16[3,3,80,320]{3,2,1,0:T(8,128)(2,1)} %conv_one.1, bf16[3,3,160,320]{3,2,1,0:T(8,128)(2,1)} %conv_two.1, bf16[160,320]{1,0:T(8,128)(2,1)} %mix_weight.1), custom_call_target="tpu_custom_call" | custom-call | tf_op jit(solution)/shard_map/block/pallas_call | solution.py:266
  54.3 1.3 %copy.6 = bf16[1,16,320]{2,1,0:T(8,128)(2,1)} copy(bf16[1,16,320]{2,1,0:T(8,128)(2,1)} %block.1) | data formatting | bytes 20480

commit v5 on v4

--- a/solution.py
+++ b/solution.py
@@ -65,11 +65,12 @@
 
     for k in FAR:
         greet(at_y(k))
-        greet(at_z(k))
     for k in (2, 1, 3):
         greet(at_x(k, core))
         greet(at_x(k, 1 - core))
     greet(partner)
+    for k in FAR:
+        greet(at_z(k))
 
     loads = [
         pltpu.make_async_copy(images.at[:, pl.ds(pl.multiple_of((1 - par) * 1024, 1024), 1024)], maps.at[0], load_sem.at[0]),

time: 55.8 us -> 56.7 us (1.016)
  Pallas kernels: 54.3 us -> 55.2 us
    pallas_call x1, Pallas kernels: 54.3 us -> 55.2 us  [step(): pl.pallas_call(kernel, out_shape=jax.ShapeDtypeStruct((1, *CHUNK), BF16),...]
where the time goes in v5:
time: 56.7 us; the launch traced here: 56.6 us
  Pallas kernels  55.2 us (97%)
  local copies, waits for them, and re-layouts  1.31 us (2%)
    pallas_call x1, Pallas kernels, step(): pl.pallas_call(kernel, out_shape=jax.ShapeDtypeStruct((1, *CHUNK), BF16),...  55.2 us
    unnamed x1, local copies, waits for them, and re-layouts  1.31 us

profile of v5, /device:TPU:1, one launch (start us, length us, event | category | flops | bytes accessed | tf_op | source)
XLA Modules:
  0.0 56.6 jit_solution(14456120490177922802)
XLA Ops:
  0.0 55.2 %block.1 = bf16[1,16,320]{2,1,0:T(8,128)(2,1)} custom-call(bf16[80,2048]{1,0:T(8,128)(2,1)} %images.1, bf16[3,3,80,320]{3,2,1,0:T(8,128)(2,1)} %conv_one.1, bf16[3,3,160,320]{3,2,1,0:T(8,128)(2,1)} %conv_two.1, bf16[160,320]{1,0:T(8,128)(2,1)} %mix_weight.1), custom_call_target="tpu_custom_call" | custom-call | tf_op jit(solution)/shard_map/block/pallas_call | solution.py:267
  55.2 1.3 %copy.6 = bf16[1,16,320]{2,1,0:T(8,128)(2,1)} copy(bf16[1,16,320]{2,1,0:T(8,128)(2,1)} %block.1) | data formatting | bytes 20480
